TPU v7x, 32 devices: a whole 2x2x4 slice. The times are simulated.
32 devices in a mesh: groups: 2 (over y), space: 4 (over z), tangent: 4 (over x, core).
Axes of the slice: x: 2, y: 2, z: 4, core: 2. Of those that a mesh axis runs over, the one named last changes fastest.
Arguments:
- positions: float32 [16, 2, 128], P(('groups', 'space')), parts along dimension 0, may hold values from 0.45 to 15.55, as said below
- momenta: float32 [16, 2, 128], P(('groups', 'space')), parts along dimension 0, may hold values from -4 to 4
- cell_count: int32 [16], P(('groups', 'space')), parts along dimension 0, may hold values from 64 to 128, as said below
- tangent: float32 [16, 4, 128, 1024], P(('groups', 'space'), None, None, 'tangent'), parts along dimension 0, may hold values from -6 to 6
Outputs:
- phase: float32 [16, 4, 128], P(('groups', 'space')), parts along dimension 0
- new_tangent: float32 [16, 4, 128, 1024], P(('groups', 'space'), None, None, 'tangent'), parts along dimension 0
- stretch: float32 [2048], P(('groups', 'tangent')), parts along dimension 0
There are 2 independent parts, one for each index of `groups`. A program takes and returns all parts, laid end to end along the dimension named above; each array names one. Nothing has to cross between parts.
Inputs may be any that keep to these rules, and one draw needn't show every extreme that they name: Slots 0 to cell_count - 1 of a cell hold particles, the others are padding; some cell holds 128 particles in every draw. `positions`: every slot of a cell, padding too, lies within 0.05 in each coordinate of its own point of the lattice (m + 0.5, n + 0.5), m from 0 to 7, n from 0 to 15; no two slots of a cell share a lattice point.
All inputs are finite; a program needn't handle non-finite values.
Results may differ from a plain program's by a relative error of at most 0.006.
Values may be sent and summed in bfloat16 or wider, within the bound.
No kernel may reach another device: no remote copies, remote signals or barrier semaphores. Data moves between devices by JAX's collectives and lax.ppermute only.
A program may use at most 128 MiB of HBM per device.

v0:
```python
import jax
import jax.numpy as jnp
from jax import lax
from jax.sharding import PartitionSpec as P

STEPS = 2
DT = 0.005
CUT2 = 2.0 ** (1.0 / 3.0)
PARK = 1000.0
HIGH = lax.Precision.HIGHEST


def padded(block, sides, width):
    for axis, dim in sides:
        count = lax.axis_size(axis)
        forward = [(i, i + 1) for i in range(count - 1)]
        forward.append((count - 1, 0))
        backward = [(target, source) for source, target in forward]
        low = lax.ppermute(
            lax.slice_in_dim(block, block.shape[dim] - width, None, axis=dim), axis, forward
        )
        high = lax.ppermute(lax.slice_in_dim(block, 0, width, axis=dim), axis, backward)
        block = jnp.concatenate([low, block, high], axis=dim)
    return block


def pair_terms(own_coords, own_alive, far_coords, shift_x, shift_y, same_cell):
    delta_x = shift_x + far_coords[:, 0, None, :] - own_coords[:, 0, :, None]
    delta_y = shift_y + far_coords[:, 1, None, :] - own_coords[:, 1, :, None]
    dist2 = delta_x * delta_x + delta_y * delta_y
    within = jnp.logical_and(dist2 < CUT2, own_alive[:, :, None] > 0.5)
    if same_cell:
        within = jnp.logical_and(within, jnp.logical_not(jnp.eye(dist2.shape[-1], dtype=bool)))
    weight = within.astype(jnp.float32)
    safe = jnp.where(within, dist2, CUT2)
    inverse = 1.0 / safe
    inv_three = inverse * inverse * inverse
    inv_six = inv_three * inv_three
    energy = 4.0 * (inv_six - inv_three) + 1.0
    energy_1 = 4.0 * (3.0 * inv_three - 6.0 * inv_six) * inverse
    energy_2 = 4.0 * (42.0 * inv_six - 12.0 * inv_three) * inverse * inverse
    taper = 1.0 - safe / CUT2
    switch = taper * taper
    switch_1 = -2.0 * taper / CUT2
    switch_2 = 2.0 / (CUT2 * CUT2)
    grad_1 = (energy_1 * switch + energy * switch_1) * weight
    grad_2 = (energy_2 * switch + 2.0 * energy_1 * switch_1 + energy * switch_2) * weight
    pull_x = 2.0 * grad_1 * delta_x
    pull_y = 2.0 * grad_1 * delta_y
    k_xx = (2.0 * grad_1 + 4.0 * grad_2 * delta_x * delta_x).astype(jnp.bfloat16)
    k_xy = (4.0 * grad_2 * delta_x * delta_y).astype(jnp.bfloat16)
    k_yy = (2.0 * grad_1 + 4.0 * grad_2 * delta_y * delta_y).astype(jnp.bfloat16)
    return (pull_x, pull_y, k_xx, k_xy, k_yy)


def apply_rows(k_xx, k_xy, k_yy, far_low):
    gain_x = jnp.einsum(
        "cij,cjv->civ", k_xx, far_low[:, 0], preferred_element_type=jnp.float32
    ) + jnp.einsum("cij,cjv->civ", k_xy, far_low[:, 1], preferred_element_type=jnp.float32)
    gain_y = jnp.einsum(
        "cij,cjv->civ", k_xy, far_low[:, 0], preferred_element_type=jnp.float32
    ) + jnp.einsum("cij,cjv->civ", k_yy, far_low[:, 1], preferred_element_type=jnp.float32)
    return (gain_x, gain_y)


def add_pair(totals, parked, occupied, far_coords, far_low, shift_x, shift_y, same_cell):
    forces_x, forces_y, push_x, push_y, diag_xx, diag_xy, diag_yy = totals
    pull_x, pull_y, k_xx, k_xy, k_yy = pair_terms(
        parked, occupied, far_coords, shift_x, shift_y, same_cell
    )
    gain_x, gain_y = apply_rows(k_xx, k_xy, k_yy, far_low)
    totals = (
        forces_x + jnp.sum(pull_x, axis=2),
        forces_y + jnp.sum(pull_y, axis=2),
        push_x + gain_x,
        push_y + gain_y,
        diag_xx + jnp.sum(k_xx.astype(jnp.float32), axis=2),
        diag_xy + jnp.sum(k_xy.astype(jnp.float32), axis=2),
        diag_yy + jnp.sum(k_yy.astype(jnp.float32), axis=2),
    )
    return (totals, (pull_x, pull_y, k_xx, k_xy, k_yy))


def evaluate(coords, occupied, small_q):
    cell_total = coords.shape[0]
    low = small_q.astype(jnp.bfloat16)
    parked = jnp.concatenate(
        [coords[:, 0:1] + PARK * (1.0 - occupied)[:, None, :], coords[:, 1:2]], axis=1
    )
    empty_rows = jnp.zeros(occupied.shape, jnp.float32)
    empty_push = jnp.zeros(small_q[:, 0].shape, jnp.float32)
    totals = (empty_rows, empty_rows, empty_push, empty_push, empty_rows, empty_rows, empty_rows)
    far_low = padded(low, (("space", 0),), cell_total)
    far_coords = padded(parked, (("space", 0),), cell_total)
    for side in (-1, 0, 1):
        if side == 0:
            block_low = low
            block_coords = parked
        else:
            begin = (1 + side) * cell_total
            block_low = far_low[begin : begin + cell_total]
            block_coords = far_coords[begin : begin + cell_total]
        for lane in (-1, 0, 1):
            totals, unused = add_pair(
                totals,
                parked,
                occupied,
                jnp.roll(block_coords, -lane, axis=0),
                jnp.roll(block_low, -lane, axis=0),
                8.0 * side,
                16.0 * lane,
                side == 0 and lane == 0,
            )
    forces_x, forces_y, push_x, push_y, diag_xx, diag_xy, diag_yy = totals
    wide_own = low.astype(jnp.float32)
    push_x = push_x - diag_xx[..., None] * wide_own[:, 0] - diag_xy[..., None] * wide_own[:, 1]
    push_y = push_y - diag_xy[..., None] * wide_own[:, 0] - diag_yy[..., None] * wide_own[:, 1]
    forces = jnp.stack([forces_x, forces_y], axis=1)
    pushes = jnp.stack([push_x, push_y], axis=1)
    return (forces, pushes)


def body(positions, momenta, cell_count, tangent):
    cell_total = positions.shape[0]
    slot_count = positions.shape[2]
    block_cols = tangent.shape[3]
    occupied = (
        lax.broadcasted_iota(jnp.int32, (cell_total, slot_count), 1) < cell_count[:, None]
    ).astype(jnp.float32)
    state = tangent * occupied[:, None, :, None]
    coords = positions
    speeds = momenta
    small_q = state[:, 0:2]
    small_p = state[:, 2:4]
    forces, pushes = evaluate(coords, occupied, small_q)
    for step_index in range(STEPS):
        midway_p = speeds + 0.5 * DT * forces
        midway_dp = small_p + 0.5 * DT * pushes
        coords = coords + DT * midway_p
        small_q = small_q + DT * midway_dp
        forces, pushes = evaluate(coords, occupied, small_q)
        speeds = midway_p + 0.5 * DT * forces
        small_p = midway_dp + 0.5 * DT * pushes
    phase = jnp.concatenate([coords, speeds], axis=1)
    final = jnp.concatenate([small_q, small_p], axis=1)
    rows_form = lax.all_to_all(final, "tangent", split_axis=2, concat_axis=3, tiled=True)
    full_width = rows_form.shape[3]
    flat_rows = rows_form.reshape(-1, full_width)
    partial_value = lax.dot_general(
        flat_rows,
        flat_rows,
        (((0,), (0,)), ((), ())),
        precision=HIGH,
        preferred_element_type=jnp.float32,
    )
    gram_scale = 1.0 / (4.0 * slot_count * cell_total * lax.axis_size("space"))
    gram = lax.psum(partial_value, ("space", "tangent"))
    factor = jnp.linalg.cholesky(gram * gram_scale)
    solved = jax.scipy.linalg.solve_triangular(factor, flat_rows.T, lower=True).T
    columns_out = lax.all_to_all(
        solved.reshape(rows_form.shape), "tangent", split_axis=3, concat_axis=2, tiled=True
    )
    log_diag = jnp.log(jnp.diagonal(factor))
    stretch = lax.dynamic_slice_in_dim(log_diag, lax.axis_index("tangent") * block_cols, block_cols)
    return (phase, columns_out, stretch)


def solution(mesh):
    placed = (
        P(("groups", "space"), None, None),
        P(("groups", "space"), None, None),
        P(("groups", "space")),
        P(("groups", "space"), None, None, "tangent"),
    )
    return jax.shard_map(
        body,
        mesh=mesh,
        in_specs=placed,
        out_specs=(
            P(("groups", "space"), None, None),
            P(("groups", "space"), None, None, "tangent"),
            P(("groups", "tangent")),
        ),
        check_vma=False,
    )
```

profile of v0, /device:TPU:1, one launch (start us, length us, event | category | flops | bytes accessed | tf_op | source)
XLA Modules:
  0.0 639.7 jit_solution(17771305510368086692)
XLA Ops:
  8.1 4.2 collective-permute-start.1
  14.4 3.3 collective-permute-start.7
  20.4 3.1 convert_reduce_fusion.79
  23.7 3.3 collective-permute-start.3
  27.9 3.4 collective-permute-done.2
  31.3 3.1 convert_reduce_fusion.52
  39.3 3.3 convert_reduce_fusion.25
  59.8 4.8 collective-permute-done.9
  82.1 2.7 collective-permute-done.11
  86.5 7.0 %collective-permute-done.10 = bf16[2,2,128,256]{3,2,0,1:T(8,128)(2,1)S(1)} collective-permute-done((bf16[2,2,128,256]{3,2,0,1:T(8,128)(2,1)S(1)}, bf16[2,2,128,256]{3,2,0,1:T(8,128)(2,1)S(1)}, u32[]{:S(2)}, u32[]{:S(2)}) %collective-permute-start.10) | collective-permute-done | bytes 262176 | tf_op jit(solution)/shard_map/ppermute | solution.py:19
  105.5 21.8 %all_to_all.33 = f32[2,4,128,256]{3,0,1,2:T(2,128)S(1)} all-to-all(f32[2,4,128,256]{3,0,1,2:T(2,128)S(1)} %copy.18), channel_id=1, replica_groups=mesh['groups'=2,'space'=4,'tangent'=4] {'tangent'}, dimensions={2} | all-to-all | bytes 2097152 | tf_op jit(solution)/shard_map/all_to_all | solution.py:146
  128.2 5.2 fusion.2420
  133.8 107.8 %all-reduce.3.cloned.1.call-done = f32[1024,1024]{0,1:T(8,128)} async-done(((f32[1024,1024]{0,1:T(8,128)}), f32[1024,1024]{0,1:T(8,128)}) %all-reduce.3.cloned.1.call-update) | async-done | bytes 4194320 | tf_op jit(solution)/shard_map/psum | solution.py:157
  241.6 5.0 broadcast_multiply_fusion
  246.6 5.7 copy.21
  252.3 4.4 fusion
  258.7 11.7 %cholesky.187 = f32[128,128]{1,0:T(8,128)S(1)} custom-call(f32[128,128]{1,0:T(8,128)S(1)} %cholesky.514), custom_call_target="Cholesky" | custom-call | tf_op jit(solution)/shard_map/jit(cholesky)/cholesky | solution.py:158
  271.1 9.8 %custom-call.63 = f32[1,128,128]{1,2,0:T(8,128)S(1)} custom-call(f32[1,128,128]{2,1,0:T(8,128)S(1)} %get-tuple-element.432), custom_call_target="InvertDiagBlocksLowerTriangular" | custom-call | tf_op jit(solution)/shard_map/jit(cholesky)/cholesky | solution.py:158
  280.9 2.5 cholesky.218
  283.4 2.3 constant_dynamic-update-slice_fusion.32
  287.3 11.9 %cholesky.209 = f32[128,128]{1,0:T(8,128)S(1)} custom-call(f32[128,128]{1,0:T(8,128)S(1)} %cholesky.518), custom_call_target="Cholesky" | custom-call | tf_op jit(solution)/shard_map/jit(cholesky)/cholesky | solution.py:158
  300.5 9.8 %custom-call.64 = f32[1,128,128]{1,2,0:T(8,128)S(1)} custom-call(f32[1,128,128]{2,1,0:T(8,128)S(1)} %get-tuple-element.429), custom_call_target="InvertDiagBlocksLowerTriangular" | custom-call | tf_op jit(solution)/shard_map/jit(cholesky)/cholesky | solution.py:158
  313.6 11.7 %cholesky.402 = f32[128,128]{1,0:T(8,128)S(1)} custom-call(f32[128,128]{1,0:T(8,128)S(1)} %cholesky.523), custom_call_target="Cholesky" | custom-call | tf_op jit(solution)/shard_map/jit(cholesky)/cholesky | solution.py:158
  326.6 9.8 %custom-call.65 = f32[1,128,128]{1,2,0:T(8,128)S(1)} custom-call(f32[1,128,128]{2,1,0:T(8,128)S(1)} %get-tuple-element.426), custom_call_target="InvertDiagBlocksLowerTriangular" | custom-call | tf_op jit(solution)/shard_map/jit(cholesky)/cholesky | solution.py:158
  337.6 2.4 convolution_subtract_fusion.2
  340.0 11.9 %cholesky.421 = f32[128,128]{1,0:T(8,128)S(1)} custom-call(f32[128,128]{1,0:T(8,128)S(1)} %cholesky.528), custom_call_target="Cholesky" | custom-call | tf_op jit(solution)/shard_map/jit(cholesky)/cholesky | solution.py:158
  353.3 9.8 %custom-call.66 = f32[1,128,128]{1,2,0:T(8,128)S(1)} custom-call(f32[1,128,128]{2,1,0:T(8,128)S(1)} %get-tuple-element.423), custom_call_target="InvertDiagBlocksLowerTriangular" | custom-call | tf_op jit(solution)/shard_map/jit(cholesky)/cholesky | solution.py:158
  364.2 2.3 convolution_subtract_fusion.3
  366.5 11.7 %cholesky.440 = f32[128,128]{1,0:T(8,128)S(1)} custom-call(f32[128,128]{1,0:T(8,128)S(1)} %cholesky.533), custom_call_target="Cholesky" | custom-call | tf_op jit(solution)/shard_map/jit(cholesky)/cholesky | solution.py:158
  379.6 10.2 %custom-call.67 = f32[1,128,128]{1,2,0:T(8,128)S(1)} custom-call(f32[1,128,128]{2,1,0:T(8,128)S(1)} %get-tuple-element.420), custom_call_target="InvertDiagBlocksLowerTriangular" | custom-call | tf_op jit(solution)/shard_map/jit(cholesky)/cholesky | solution.py:158
  390.8 2.3 convolution_subtract_fusion.4
  393.1 11.7 %cholesky.460 = f32[128,128]{1,0:T(8,128)S(1)} custom-call(f32[128,128]{1,0:T(8,128)S(1)} %cholesky.538), custom_call_target="Cholesky" | custom-call | tf_op jit(solution)/shard_map/jit(cholesky)/cholesky | solution.py:158
  406.1 9.8 %custom-call.68 = f32[1,128,128]{1,2,0:T(8,128)S(1)} custom-call(f32[1,128,128]{2,1,0:T(8,128)S(1)} %get-tuple-element.417), custom_call_target="InvertDiagBlocksLowerTriangular" | custom-call | tf_op jit(solution)/shard_map/jit(cholesky)/cholesky | solution.py:158
  418.9 11.9 %cholesky.480 = f32[128,128]{1,0:T(8,128)S(1)} custom-call(f32[128,128]{1,0:T(8,128)S(1)} %cholesky.543), custom_call_target="Cholesky" | custom-call | tf_op jit(solution)/shard_map/jit(cholesky)/cholesky | solution.py:158
  432.1 9.8 %custom-call.69 = f32[1,128,128]{1,2,0:T(8,128)S(1)} custom-call(f32[1,128,128]{2,1,0:T(8,128)S(1)} %get-tuple-element.414), custom_call_target="InvertDiagBlocksLowerTriangular" | custom-call | tf_op jit(solution)/shard_map/jit(cholesky)/cholesky | solution.py:158
  444.5 11.7 %cholesky.498 = f32[128,128]{1,0:T(8,128)S(1)} custom-call(f32[128,128]{1,0:T(8,128)S(1)} %convolution_subtract_fusion.13), custom_call_target="Cholesky" | custom-call | tf_op jit(solution)/shard_map/jit(cholesky)/cholesky | solution.py:158
  462.6 6.6 %fusion.1 = (f32[1024,1024]{1,0:T(8,128)}, f32[1024,1024]{1,0:T(8,128)}) fusion(f32[1024,1024]{1,0:T(8,128)} %get-tuple-element.412, pred[]{:T(512)S(6)} %cholesky.513), kind=kLoop, calls=%fused_computation.7 | loop fusion | flops 4194304 | bytes 12582913 | tf_op jit(solution)/shard_map/jit(_solve_triangular)/triangular_solve | solution.py:159
  469.2 23.2 %while.1 = (s32[]{:T(128)}, f32[1024,1024]{1,0:T(8,128)}, s32[8,2]{0,1:T(2,128)S(1)}, f32[8,128,128]{2,1,0:T(8,128)S(1)}, s32[]{:T(128)}) while((s32[]{:T(128)}, f32[1024,1024]{1,0:T(8,128)}, s32[8,2]{0,1:T(2,128)S(1)}, f32[8,128,128]{2,1,0:T(8,128)S(1)}, s32[]{:T(128)}) %tuple.396), condition=%wide.while_cond, body=%wide.while_body.sunk | while | flops 2 | bytes 131189 | solution.py:159
  469.8 2.3 bitcast_dynamic-update-slice_fusion.2
  472.7 2.3 bitcast_dynamic-update-slice_fusion.2
  492.4 79.4 %custom-call.70 = f32[8,128,128]{1,2,0:T(8,128)} custom-call(f32[8,128,128]{2,1,0:T(8,128)S(1)} %get-tuple-element.10), custom_call_target="InvertDiagBlocksLowerTriangular" | custom-call | tf_op jit(solution)/shard_map/jit(_solve_triangular)/triangular_solve | solution.py:159
  587.0 3.1 copy.24
  590.1 5.3 reshape.847
  595.5 5.5 all-to-all-start.1
  601.7 17.3 %gather_fusion = f32[1024]{0:T(1024)S(1)} fusion(f32[1024,1024]{1,0:T(8,128)} %get-tuple-element.320, s32[1024]{0:T(1024)S(1)} %bitcast.397), kind=kCustom, calls=%fused_computation | custom fusion | bytes 16384 | tf_op jit(solution)/shard_map/jit(diagonal)/cond/branch_0_fun/gather | solution.py:163
  620.2 3.7 reduce.48
  623.8 4.2 reshape.848
  628.1 4.6 copy.25
  (302 shorter events, 121.6 us)
Async XLA Ops:
  7.2 234.4 %all-reduce.3.cloned.1.call-start = ((), (), s32[]{:S(2)}) async-start(), calls=%async_computation.2 | async-start | bytes 8388608 | tf_op jit(solution)/shard_map/psum | solution.py:157
  8.1 12.2 %collective-permute-start.1 = (f32[2,2,128]{2,1,0:T(2,128)S(1)}, f32[2,2,128]{2,1,0:T(2,128)S(1)}, u32[]{:S(2)}, u32[]{:S(2)}) collective-permute-start(f32[2,2,128]{2,1,0:T(2,128)S(1)} %pad_maximum_fusion.11), channel_id=1, source_target_pairs={{4,0},{8,4},{12,8},{0,12},{5,1},{9,5},{13,9},{1,13},{6,2},{10,6},{... | collective-permute-start | bytes 6152 | tf_op jit(solution)/shard_map/ppermute | solution.py:22
  12.3 8.1 %collective-permute-start = (f32[2,2,128]{2,1,0:T(2,128)S(1)}, f32[2,2,128]{2,1,0:T(2,128)S(1)}, u32[]{:S(2)}, u32[]{:S(2)}) collective-permute-start(f32[2,2,128]{2,1,0:T(2,128)S(1)} %pad_maximum_fusion.11), channel_id=1, source_target_pairs={{0,4},{4,8},{8,12},{12,0},{1,5},{5,9},{9,13},{13,1},{2,6},{6,10},{... | collective-permute-start | bytes 6152 | tf_op jit(solution)/shard_map/ppermute | solution.py:19
  14.4 28.2 %collective-permute-start.7 = (bf16[2,2,128,256]{3,2,0,1:T(8,128)(2,1)S(1)}, bf16[2,2,128,256]{3,2,0,1:T(8,128)(2,1)S(1)}, u32[]{:S(2)}, u32[]{:S(2)}) collective-permute-start(bf16[2,2,128,256]{3,2,0,1:T(8,128)(2,1)S(1)} %get-tuple-element.327), channel_id=1, source_target_pairs={{4,0},{8,4},{12,8},{0,12},{5,1},{9,5},{13,9},{1,13},{6,2},{10,6},{... | collective-permute-start | bytes 786440 | tf_op jit(solution)/shard_map/ppermute | solution.py:22
  17.7 26.6 %collective-permute-start.6 = (bf16[2,2,128,256]{3,2,0,1:T(8,128)(2,1)S(1)}, bf16[2,2,128,256]{3,2,0,1:T(8,128)(2,1)S(1)}, u32[]{:S(2)}, u32[]{:S(2)}) collective-permute-start(bf16[2,2,128,256]{3,2,0,1:T(8,128)(2,1)S(1)} %get-tuple-element.327), channel_id=1, source_target_pairs={{0,4},{4,8},{8,12},{12,0},{1,5},{5,9},{9,13},{13,1},{2,6},{6,10},{... | collective-permute-start | bytes 786440 | tf_op jit(solution)/shard_map/ppermute | solution.py:19
  18.6 4.9 copy-start.3
  18.6 4.9 copy-start.4
  18.7 4.9 copy-start.2
  23.7 4.2 collective-permute-start.3
  27.0 4.2 collective-permute-start.2
  34.6 2.5 collective-permute-start.5
  35.0 4.2 collective-permute-start.4
  57.1 7.5 %collective-permute-start.9 = (bf16[2,2,128,256]{3,2,0,1:T(8,128)(2,1)S(1)}, bf16[2,2,128,256]{3,2,0,1:T(8,128)(2,1)S(1)}, u32[]{:S(2)}, u32[]{:S(2)}) collective-permute-start(bf16[2,2,128,256]{3,2,0,1:T(8,128)(2,1)S(1)} %get-tuple-element.325), channel_id=1, source_target_pairs={{4,0},{8,4},{12,8},{0,12},{5,1},{9,5},{13,9},{1,13},{6,2},{10,6},{... | collective-permute-start | bytes 786440 | tf_op jit(solution)/shard_map/ppermute | solution.py:22
  58.0 8.5 %collective-permute-start.8 = (bf16[2,2,128,256]{3,2,0,1:T(8,128)(2,1)S(1)}, bf16[2,2,128,256]{3,2,0,1:T(8,128)(2,1)S(1)}, u32[]{:S(2)}, u32[]{:S(2)}) collective-permute-start(bf16[2,2,128,256]{3,2,0,1:T(8,128)(2,1)S(1)} %get-tuple-element.325), channel_id=1, source_target_pairs={{0,4},{4,8},{8,12},{12,0},{1,5},{5,9},{9,13},{13,1},{2,6},{6,10},{... | collective-permute-start | bytes 786440 | tf_op jit(solution)/shard_map/ppermute | solution.py:19
  79.4 5.5 collective-permute-start.11
  80.8 12.8 %collective-permute-start.10 = (bf16[2,2,128,256]{3,2,0,1:T(8,128)(2,1)S(1)}, bf16[2,2,128,256]{3,2,0,1:T(8,128)(2,1)S(1)}, u32[]{:S(2)}, u32[]{:S(2)}) collective-permute-start(bf16[2,2,128,256]{3,2,0,1:T(8,128)(2,1)S(1)} %get-tuple-element.322), channel_id=1, source_target_pairs={{0,4},{4,8},{8,12},{12,0},{1,5},{5,9},{9,13},{13,1},{2,6},{6,10},{... | collective-permute-start | bytes 786440 | tf_op jit(solution)/shard_map/ppermute | solution.py:19
  256.8 1.9 copy-start
  571.8 7.2 %copy-start.1 = (f32[8,128,128]{1,2,0:T(8,128)S(1)}, f32[8,128,128]{1,2,0:T(8,128)}, u32[]{:S(2)}) copy-start(f32[8,128,128]{1,2,0:T(8,128)} %custom-call.70) | copy-start | bytes 1572868
  595.5 24.2 %all-to-all-start.1 = ((f32[4,1,65536]{2,1,0:T(1,128)}), f32[4,1,65536]{2,1,0:T(1,128)S(1)}, u32[]{:S(2)}, u32[]{:S(2)}) async-start(f32[4,1,65536]{2,1,0:T(1,128)} %reshape.847), calls=%async_computation.1 | async-start | bytes 2097152 | tf_op jit(solution)/shard_map/all_to_all | solution.py:160
Sparse Core Ops, SparseCore 0:
  133.6 107.9 all-reduce.2
where the time goes:
time: 647 us; the launch traced here: 640 us
  other arithmetic  287 us (44%)
  waiting for transfers between devices  130 us (20%)
  matrix products  87.6 us (14%)
  local copies, waits for them, and re-layouts  71.5 us (11%)
  starting transfers between devices  21.9 us (3%)
  blocking collectives  21.8 us (3%)
  between operations  20.3 us (3%)
    another operation x31, other arithmetic, body(): factor = jnp.linalg.cholesky(gram * gram_scale)  173 us
    psum x1, waiting for transfers between devices, body(): gram = lax.psum(partial_value, ('space', 'tangent'))  108 us
    another operation x3, other arithmetic, body(): jax.scipy.linalg.solve_triangular(factor, flat_rows.T, lower=True)  86 us
    another operation x14, matrix products, body(): factor = jnp.linalg.cholesky(gram * gram_scale)  23.1 us
    another operation x24, local copies, waits for them, and re-layouts  23 us
    all_to_all x1, blocking collectives, body(): lax.all_to_all(final, 'tangent', split_axis=2, concat_axis=3, tiled=True)  21.8 us
    gather x1, local copies, waits for them, and re-layouts, body(): log_diag = jnp.log(jnp.diagonal(factor))  17.3 us
    another operation x15, matrix products, body(): jax.scipy.linalg.solve_triangular(factor, flat_rows.T, lower=True)  14.7 us
  transfers between devices with their start and end apart: 14, of which 9 were waited for; matrix products, arithmetic and copies ran while one was open for 6% of the time, Pallas kernels for 0%

commit v1 on v0

--- a/solution.py
+++ b/solution.py
@@ -2,12 +2,17 @@
 import jax.numpy as jnp
 from jax import lax
 from jax.sharding import PartitionSpec as P
+from jax.lax import all_gather
 
 STEPS = 2
 DT = 0.005
 CUT2 = 2.0 ** (1.0 / 3.0)
 PARK = 1000.0
 HIGH = lax.Precision.HIGHEST
+
+
+def clear_forms(a0, across):
+    return jnp.sum(all_gather(a0, across), axis=0)
 
 
 def padded(block, sides, width):
@@ -154,7 +159,7 @@
         preferred_element_type=jnp.float32,
     )
     gram_scale = 1.0 / (4.0 * slot_count * cell_total * lax.axis_size("space"))
-    gram = lax.psum(partial_value, ("space", "tangent"))
+    gram = clear_forms(partial_value, ("space", "tangent"))
     factor = jnp.linalg.cholesky(gram * gram_scale)
     solved = jax.scipy.linalg.solve_triangular(factor, flat_rows.T, lower=True).T
     columns_out = lax.all_to_all(

time: 647 us -> 874 us (1.35)
  waiting for transfers between devices: 130 us -> 341 us
  other arithmetic: 287 us -> 304 us
    all_gather x0 -> x1, waiting for transfers between devices: none -> 325 us  [clear_forms(): return jnp.sum(all_gather(a0, across), axis=0)]
    psum x1 -> x0, waiting for transfers between devices: 108 us -> none  [body(): gram = lax.psum(partial_value, ('space', 'tangent'))]
    reduce_sum x0 -> x1, other arithmetic: none -> 22.9 us  [clear_forms(): return jnp.sum(all_gather(a0, across), axis=0)]
  transfers between devices with their start and end apart: 14 -> 14, of which waited for: 9 -> 7; matrix products, arithmetic and copies ran while one was open for 6% -> 5% of each run, Pallas kernels for 0% -> 0%
where the time goes in v1:
time: 874 us; the launch traced here: 867 us
  waiting for transfers between devices  341 us (39%)
  other arithmetic  304 us (35%)
  matrix products  87.6 us (10%)
  local copies, waits for them, and re-layouts  71.5 us (8%)
  starting transfers between devices  22.2 us (3%)
  between operations  20.4 us (2%)
  blocking collectives  19.7 us (2%)
    all_gather x1, waiting for transfers between devices, clear_forms(): return jnp.sum(all_gather(a0, across), axis=0)  325 us
    another operation x31, other arithmetic, body(): factor = jnp.linalg.cholesky(gram * gram_scale)  173 us
    another operation x3, other arithmetic, body(): jax.scipy.linalg.solve_triangular(factor, flat_rows.T, lower=True)  86 us
    another operation x14, matrix products, body(): factor = jnp.linalg.cholesky(gram * gram_scale)  23.1 us
    another operation x24, local copies, waits for them, and re-layouts  23 us
    reduce_sum x1, other arithmetic, clear_forms(): return jnp.sum(all_gather(a0, across), axis=0)  22.9 us
    all_to_all x1, blocking collectives, body(): lax.all_to_all(final, 'tangent', split_axis=2, concat_axis=3, tiled=True)  19.7 us
  transfers between devices with their start and end apart: 14, of which 7 were waited for; matrix products, arithmetic and copies ran while one was open for 5% of the time, Pallas kernels for 0%

profile of v1, /device:TPU:1, one launch (start us, length us, event | category | flops | bytes accessed | tf_op | source)
XLA Modules:
  0.0 866.9 jit_solution(14498308853528486400)
XLA Ops:
  18.6 3.1 convert_reduce_fusion.79
  22.0 3.3 collective-permute-start.3
  26.9 3.1 convert_reduce_fusion.52
  34.5 3.1 convert_reduce_fusion.25
  50.5 3.5 collective-permute-start.9
  56.9 7.1 collective-permute-done.8
  81.0 7.2 collective-permute-done.10
  101.9 19.7 %all_to_all.33 = f32[2,4,128,256]{3,0,1,2:T(2,128)S(1)} all-to-all(f32[2,4,128,256]{3,0,1,2:T(2,128)S(1)} %copy.16), channel_id=1, replica_groups=mesh['groups'=2,'space'=4,'tangent'=4] {'tangent'}, dimensions={2} | all-to-all | bytes 2097152 | tf_op jit(solution)/shard_map/all_to_all | solution.py:151
  122.4 5.1 fusion.2420
  128.0 324.6 %all-gather.3.cloned.1.call-done = f32[16384,1024]{1,0:T(8,128)} async-done(((f32[1024,1024]{1,0:T(8,128)}), f32[16384,1024]{1,0:T(8,128)}) %all-gather.3.cloned.1.call-update) | async-done | bytes 67108880 | tf_op jit(solution)/shard_map/all_gather | solution.py:15
  452.6 22.9 %reduce_sum.1433 = f32[1024,1024]{1,0:T(8,128)} reduce(f32[16,1024,1024]{2,1,0:T(8,128)} %bitcast.101, f32[]{:T(128)} %constant.447.clone.1), dimensions={0}, to_apply=%region_135.136 | reduce | flops 15728640 | bytes 71303168 | tf_op jit(solution)/shard_map/reduce_sum | solution.py:15
  475.5 5.7 copy.18
  481.2 4.4 fusion
  487.6 11.7 %cholesky.187 = f32[128,128]{1,0:T(8,128)S(1)} custom-call(f32[128,128]{1,0:T(8,128)S(1)} %cholesky.514), custom_call_target="Cholesky" | custom-call | tf_op jit(solution)/shard_map/jit(cholesky)/cholesky | solution.py:163
  499.3 2.5 cholesky.218
  501.9 9.8 %custom-call.63 = f32[1,128,128]{1,2,0:T(8,128)S(1)} custom-call(f32[1,128,128]{2,1,0:T(8,128)S(1)} %get-tuple-element.432), custom_call_target="InvertDiagBlocksLowerTriangular" | custom-call | tf_op jit(solution)/shard_map/jit(cholesky)/cholesky | solution.py:163
  511.7 2.3 constant_dynamic-update-slice_fusion.32
  515.6 11.9 %cholesky.209 = f32[128,128]{1,0:T(8,128)S(1)} custom-call(f32[128,128]{1,0:T(8,128)S(1)} %cholesky.518), custom_call_target="Cholesky" | custom-call | tf_op jit(solution)/shard_map/jit(cholesky)/cholesky | solution.py:163
  528.1 9.8 %custom-call.64 = f32[1,128,128]{1,2,0:T(8,128)S(1)} custom-call(f32[1,128,128]{2,1,0:T(8,128)S(1)} %get-tuple-element.429), custom_call_target="InvertDiagBlocksLowerTriangular" | custom-call | tf_op jit(solution)/shard_map/jit(cholesky)/cholesky | solution.py:163
  541.3 11.7 %cholesky.402 = f32[128,128]{1,0:T(8,128)S(1)} custom-call(f32[128,128]{1,0:T(8,128)S(1)} %cholesky.523), custom_call_target="Cholesky" | custom-call | tf_op jit(solution)/shard_map/jit(cholesky)/cholesky | solution.py:163
  553.6 9.8 %custom-call.65 = f32[1,128,128]{1,2,0:T(8,128)S(1)} custom-call(f32[1,128,128]{2,1,0:T(8,128)S(1)} %get-tuple-element.426), custom_call_target="InvertDiagBlocksLowerTriangular" | custom-call | tf_op jit(solution)/shard_map/jit(cholesky)/cholesky | solution.py:163
  564.6 2.4 convolution_subtract_fusion.2
  567.0 11.9 %cholesky.421 = f32[128,128]{1,0:T(8,128)S(1)} custom-call(f32[128,128]{1,0:T(8,128)S(1)} %cholesky.528), custom_call_target="Cholesky" | custom-call | tf_op jit(solution)/shard_map/jit(cholesky)/cholesky | solution.py:163
  579.6 9.8 %custom-call.66 = f32[1,128,128]{1,2,0:T(8,128)S(1)} custom-call(f32[1,128,128]{2,1,0:T(8,128)S(1)} %get-tuple-element.423), custom_call_target="InvertDiagBlocksLowerTriangular" | custom-call | tf_op jit(solution)/shard_map/jit(cholesky)/cholesky | solution.py:163
  590.5 2.3 convolution_subtract_fusion.3
  592.8 11.7 %cholesky.440 = f32[128,128]{1,0:T(8,128)S(1)} custom-call(f32[128,128]{1,0:T(8,128)S(1)} %cholesky.533), custom_call_target="Cholesky" | custom-call | tf_op jit(solution)/shard_map/jit(cholesky)/cholesky | solution.py:163
  605.2 10.2 %custom-call.67 = f32[1,128,128]{1,2,0:T(8,128)S(1)} custom-call(f32[1,128,128]{2,1,0:T(8,128)S(1)} %get-tuple-element.420), custom_call_target="InvertDiagBlocksLowerTriangular" | custom-call | tf_op jit(solution)/shard_map/jit(cholesky)/cholesky | solution.py:163
  616.4 2.3 convolution_subtract_fusion.4
  618.7 11.7 %cholesky.460 = f32[128,128]{1,0:T(8,128)S(1)} custom-call(f32[128,128]{1,0:T(8,128)S(1)} %cholesky.538), custom_call_target="Cholesky" | custom-call | tf_op jit(solution)/shard_map/jit(cholesky)/cholesky | solution.py:163
  631.1 9.8 %custom-call.68 = f32[1,128,128]{1,2,0:T(8,128)S(1)} custom-call(f32[1,128,128]{2,1,0:T(8,128)S(1)} %get-tuple-element.417), custom_call_target="InvertDiagBlocksLowerTriangular" | custom-call | tf_op jit(solution)/shard_map/jit(cholesky)/cholesky | solution.py:163
  643.9 11.7 %cholesky.480 = f32[128,128]{1,0:T(8,128)S(1)} custom-call(f32[128,128]{1,0:T(8,128)S(1)} %cholesky.543), custom_call_target="Cholesky" | custom-call | tf_op jit(solution)/shard_map/jit(cholesky)/cholesky | solution.py:163
  656.3 9.8 %custom-call.69 = f32[1,128,128]{1,2,0:T(8,128)S(1)} custom-call(f32[1,128,128]{2,1,0:T(8,128)S(1)} %get-tuple-element.414), custom_call_target="InvertDiagBlocksLowerTriangular" | custom-call | tf_op jit(solution)/shard_map/jit(cholesky)/cholesky | solution.py:163
  668.7 11.7 %cholesky.498 = f32[128,128]{1,0:T(8,128)S(1)} custom-call(f32[128,128]{1,0:T(8,128)S(1)} %convolution_subtract_fusion.13), custom_call_target="Cholesky" | custom-call | tf_op jit(solution)/shard_map/jit(cholesky)/cholesky | solution.py:163
  691.4 6.6 fusion.1
  698.0 23.2 %while.1 = (s32[]{:T(128)}, f32[1024,1024]{1,0:T(8,128)}, s32[8,2]{0,1:T(2,128)S(1)}, f32[8,128,128]{2,1,0:T(8,128)S(1)}, s32[]{:T(128)}) while((s32[]{:T(128)}, f32[1024,1024]{1,0:T(8,128)}, s32[8,2]{0,1:T(2,128)S(1)}, f32[8,128,128]{2,1,0:T(8,128)S(1)}, s32[]{:T(128)}) %tuple.396), condition=%wide.while_cond, body=%wide.while_body.sunk | while | flops 2 | bytes 131189 | solution.py:164
  698.6 2.3 bitcast_dynamic-update-slice_fusion.2
  701.5 2.3 bitcast_dynamic-update-slice_fusion.2
  707.3 2.3 bitcast_dynamic-update-slice_fusion.2
  710.2 2.3 bitcast_dynamic-update-slice_fusion.2
  713.1 2.3 bitcast_dynamic-update-slice_fusion.2
  721.2 79.4 %custom-call.70 = f32[8,128,128]{1,2,0:T(8,128)} custom-call(f32[8,128,128]{2,1,0:T(8,128)S(1)} %get-tuple-element.10), custom_call_target="InvertDiagBlocksLowerTriangular" | custom-call | tf_op jit(solution)/shard_map/jit(_solve_triangular)/triangular_solve | solution.py:164
  815.8 3.1 copy.21
  818.9 5.3 reshape.848
  824.3 4.0 all-to-all-start.1
  828.9 17.3 %gather_fusion = f32[1024]{0:T(1024)S(1)} fusion(f32[1024,1024]{1,0:T(8,128)} %get-tuple-element.320, s32[1024]{0:T(1024)S(1)} %bitcast.398), kind=kCustom, calls=%fused_computation | custom fusion | bytes 16384 | tf_op jit(solution)/shard_map/jit(diagonal)/cond/branch_0_fun/gather | solution.py:168
  847.4 3.7 reduce.48
  851.1 4.2 reshape.849
  855.3 4.6 copy.22
  (302 shorter events, 118.9 us)
Async XLA Ops:
  7.2 445.4 %all-gather.3.cloned.1.call-start = ((), (), s32[]{:S(2)}) async-start(), calls=%async_computation.2 | async-start | bytes 71303168 | tf_op jit(solution)/shard_map/all_gather | solution.py:15
  8.1 10.5 %collective-permute-start = (f32[2,2,128]{2,1,0:T(2,128)S(1)}, f32[2,2,128]{2,1,0:T(2,128)S(1)}, u32[]{:S(2)}, u32[]{:S(2)}) collective-permute-start(f32[2,2,128]{2,1,0:T(2,128)S(1)} %pad_maximum_fusion.11), channel_id=1, source_target_pairs={{0,4},{4,8},{8,12},{12,0},{1,5},{5,9},{9,13},{13,1},{2,6},{6,10},{... | collective-permute-start | bytes 6152 | tf_op jit(solution)/shard_map/ppermute | solution.py:24
  10.2 8.3 collective-permute-start.1
  14.5 24.1 %collective-permute-start.7 = (bf16[2,2,128,256]{3,2,0,1:T(8,128)(2,1)S(1)}, bf16[2,2,128,256]{3,2,0,1:T(8,128)(2,1)S(1)}, u32[]{:S(2)}, u32[]{:S(2)}) collective-permute-start(bf16[2,2,128,256]{3,2,0,1:T(8,128)(2,1)S(1)} %get-tuple-element.327), channel_id=1, source_target_pairs={{4,0},{8,4},{12,8},{0,12},{5,1},{9,5},{13,9},{1,13},{6,2},{10,6},{... | collective-permute-start | bytes 786440 | tf_op jit(solution)/shard_map/ppermute | solution.py:27
  15.9 21.8 %collective-permute-start.6 = (bf16[2,2,128,256]{3,2,0,1:T(8,128)(2,1)S(1)}, bf16[2,2,128,256]{3,2,0,1:T(8,128)(2,1)S(1)}, u32[]{:S(2)}, u32[]{:S(2)}) collective-permute-start(bf16[2,2,128,256]{3,2,0,1:T(8,128)(2,1)S(1)} %get-tuple-element.327), channel_id=1, source_target_pairs={{0,4},{4,8},{8,12},{12,0},{1,5},{5,9},{9,13},{13,1},{2,6},{6,10},{... | collective-permute-start | bytes 786440 | tf_op jit(solution)/shard_map/ppermute | solution.py:24
  16.9 4.9 copy-start.3
  16.9 4.9 copy-start.4
  16.9 4.9 copy-start.2
  21.9 4.9 collective-permute-start.2
  22.0 4.1 collective-permute-start.3
  30.2 4.3 collective-permute-start.4
  31.6 2.8 collective-permute-start.5
  50.5 14.3 %collective-permute-start.9 = (bf16[2,2,128,256]{3,2,0,1:T(8,128)(2,1)S(1)}, bf16[2,2,128,256]{3,2,0,1:T(8,128)(2,1)S(1)}, u32[]{:S(2)}, u32[]{:S(2)}) collective-permute-start(bf16[2,2,128,256]{3,2,0,1:T(8,128)(2,1)S(1)} %get-tuple-element.325), channel_id=1, source_target_pairs={{4,0},{8,4},{12,8},{0,12},{5,1},{9,5},{13,9},{1,13},{6,2},{10,6},{... | collective-permute-start | bytes 786440 | tf_op jit(solution)/shard_map/ppermute | solution.py:27
  54.0 10.0 %collective-permute-start.8 = (bf16[2,2,128,256]{3,2,0,1:T(8,128)(2,1)S(1)}, bf16[2,2,128,256]{3,2,0,1:T(8,128)(2,1)S(1)}, u32[]{:S(2)}, u32[]{:S(2)}) collective-permute-start(bf16[2,2,128,256]{3,2,0,1:T(8,128)(2,1)S(1)} %get-tuple-element.325), channel_id=1, source_target_pairs={{0,4},{4,8},{8,12},{12,0},{1,5},{5,9},{9,13},{13,1},{2,6},{6,10},{... | collective-permute-start | bytes 786440 | tf_op jit(solution)/shard_map/ppermute | solution.py:24
  76.8 12.2 %collective-permute-start.11 = (bf16[2,2,128,256]{3,2,0,1:T(8,128)(2,1)S(1)}, bf16[2,2,128,256]{3,2,0,1:T(8,128)(2,1)S(1)}, u32[]{:S(2)}, u32[]{:S(2)}) collective-permute-start(bf16[2,2,128,256]{3,2,0,1:T(8,128)(2,1)S(1)} %get-tuple-element.322), channel_id=1, source_target_pairs={{4,0},{8,4},{12,8},{0,12},{5,1},{9,5},{13,9},{1,13},{6,2},{10,6},{... | collective-permute-start | bytes 786440 | tf_op jit(solution)/shard_map/ppermute | solution.py:27
  78.3 9.9 %collective-permute-start.10 = (bf16[2,2,128,256]{3,2,0,1:T(8,128)(2,1)S(1)}, bf16[2,2,128,256]{3,2,0,1:T(8,128)(2,1)S(1)}, u32[]{:S(2)}, u32[]{:S(2)}) collective-permute-start(bf16[2,2,128,256]{3,2,0,1:T(8,128)(2,1)S(1)} %get-tuple-element.322), channel_id=1, source_target_pairs={{0,4},{4,8},{8,12},{12,0},{1,5},{5,9},{9,13},{13,1},{2,6},{6,10},{... | collective-permute-start | bytes 786440 | tf_op jit(solution)/shard_map/ppermute | solution.py:24
  485.7 1.9 copy-start
  800.6 7.2 copy-start.1
  824.3 22.6 %all-to-all-start.1 = ((f32[4,1,65536]{2,1,0:T(1,128)}), f32[4,1,65536]{2,1,0:T(1,128)S(1)}, u32[]{:S(2)}, u32[]{:S(2)}) async-start(f32[4,1,65536]{2,1,0:T(1,128)} %reshape.848), calls=%async_computation.1 | async-start | bytes 2097152 | tf_op jit(solution)/shard_map/all_to_all | solution.py:165
Sparse Core Ops, SparseCore 0:
  127.7 324.8 all-gather.2
